TPU v7x, 256 devices: a whole 4x4x8 slice. The times are simulated.
256 devices in a mesh: seq: 32 (over x, y, core), cb: 8 (over z).
Axes of the slice: x: 4, y: 4, z: 8, core: 2. Of those that a mesh axis runs over, the one named last changes fastest.
Arguments:
- context: bfloat16 [16384, 2048], P('seq', 'cb'), may hold values from -6 to 6
- lengths: int32 [64], replicated, may hold values from 1 to 256, 10240 in all
- tokens: int32 [16384, 8], P('seq', 'cb'), may hold values from 0 to 2047
- masks: int32 [16384, 8], P('seq', 'cb'), may hold values 0 or 1
- w_in: bfloat16 [8, 2048, 1024], P('cb', 'seq'), may hold values from -0.125 to 0.125
- w_head: bfloat16 [8, 2048, 1024], P('cb', 'seq'), may hold values from -60 to 60
Outputs:
- loss: float32 [], replicated
- grad_context: bfloat16 [16384, 2048], P('seq', 'cb')
- grad_in: float32 [8, 2048, 1024], P('cb', 'seq')
- grad_head: float32 [8, 2048, 1024], P('cb', 'seq')
Inputs may be any that keep to these rules, and one draw needn't show every extreme that they name: The lengths sum to 10240, and the longest is exactly 256.
All inputs are finite; a program needn't handle non-finite values. No bound on the sum of `masks` on one device may be relied on, other than what follows from the above.
Results may differ from a plain program's by a relative error of at most 0.02.
Values may be sent and summed in bfloat16 or wider, within the bound.
No kernel may reach another device: no remote copies, remote signals or barrier semaphores. Data moves between devices by JAX's collectives and lax.ppermute only.
A program may use at most 128 MiB of HBM per device.

v0:
```python
import jax
import jax.numpy as jnp
from jax import lax
from jax.sharding import PartitionSpec as P

FRAMES = 256


EPS = 1e-06


def lookup(table, index):
    spots = jnp.arange(table.shape[0], dtype=jnp.int32)
    return jnp.sum(jnp.where(index[:, None] == spots[None, :], table[None, :], 0), axis=1)


def local(context, lengths, tokens, masks, w_in, w_head):
    seq_count = lax.axis_size("seq")
    cb_total = lax.axis_size("cb") * w_in.shape[0]
    seq_here = lax.axis_index("seq")
    rows_here = context.shape[0]
    streams_here = rows_here // FRAMES
    positions = jnp.arange(rows_here, dtype=jnp.int32)
    own_stream = seq_here * streams_here + positions // FRAMES
    live = positions % FRAMES < lookup(lengths, own_stream)
    labels = jnp.where(live & (masks[:, 0] > 0), tokens[:, 0], -1)
    keeps = labels >= 0
    keep_float = keeps.astype(jnp.float32)
    full_rows = lax.all_gather(context, "cb", axis=1, tiled=True)
    in_full, head_full = (
        lax.all_gather(w_in, "seq", axis=1, tiled=True),
        lax.all_gather(w_head, "seq", axis=1, tiled=True),
    )
    in_matrix = in_full[0]
    head_matrix = head_full[0]
    hidden = jnp.dot(full_rows, in_matrix, preferred_element_type=jnp.float32)
    inverse = lax.rsqrt(jnp.mean(hidden * hidden, axis=1, keepdims=True) + EPS)
    normed = hidden * inverse
    normed_bf = normed.astype(jnp.bfloat16)
    logits = lax.dot_general(
        normed_bf, head_matrix, (((1,), (1,)), ((), ())), preferred_element_type=jnp.float32
    )
    peak = jnp.max(logits, axis=1, keepdims=True)
    shifted = jnp.exp(logits - peak)
    total = jnp.sum(shifted, axis=1, keepdims=True)
    vocab_ids = jnp.arange(logits.shape[1], dtype=jnp.int32)
    target = vocab_ids[None, :] == labels[:, None]
    picked = jnp.sum(jnp.where(target, logits, 0.0), axis=1)
    entropy_terms = jnp.where(keeps, peak[:, 0] + jnp.log(total[:, 0]) - picked, 0.0)
    count = lax.psum(jnp.sum(keep_float), "seq")
    loss = lax.psum(jnp.sum(entropy_terms) / count / cb_total, ("seq", "cb"))
    rows_total = FRAMES * streams_here * seq_count
    weight = keep_float * (rows_total / (count * cb_total))
    grad_logits = ((shifted / total - target.astype(jnp.float32)) * weight[:, None]).astype(
        jnp.bfloat16
    )
    grad_normed = jnp.dot(grad_logits, head_matrix, preferred_element_type=jnp.float32)
    grad_hidden = inverse * (
        grad_normed - normed * jnp.mean(grad_normed * normed, axis=1, keepdims=True)
    )
    grad_hidden_bf = grad_hidden.astype(jnp.bfloat16)
    head_term = lax.dot_general(
        grad_logits, normed_bf, (((0,), (0,)), ((), ())), preferred_element_type=jnp.float32
    )
    in_term = lax.dot_general(
        full_rows, grad_hidden_bf, (((0,), (0,)), ((), ())), preferred_element_type=jnp.float32
    )
    head_part, in_part = (
        lax.psum_scatter(
            head_term.astype(jnp.bfloat16), "seq", scatter_dimension=0, tiled=True
        ).astype(jnp.float32),
        lax.psum_scatter(
            in_term.astype(jnp.bfloat16), "seq", scatter_dimension=0, tiled=True
        ).astype(jnp.float32),
    )
    context_term = lax.dot_general(
        grad_hidden_bf, in_matrix, (((1,), (1,)), ((), ())), preferred_element_type=jnp.float32
    )
    context_part = lax.psum_scatter(context_term, "cb", scatter_dimension=1, tiled=True).astype(
        jnp.bfloat16
    )
    return (loss, context_part, in_part[None], head_part[None])


def solution(mesh):
    in_specs = (
        P("seq", "cb"),
        P(),
        P("seq", "cb"),
        P("seq", "cb"),
        P("cb", "seq", None),
        P("cb", "seq", None),
    )
    out_specs = (P(), P("seq", "cb"), P("cb", "seq", None), P("cb", "seq", None))
    return jax.shard_map(local, mesh=mesh, in_specs=in_specs, out_specs=out_specs, check_vma=False)
```

profile of v0, /device:TPU:24, one launch (start us, length us, event | category | flops | bytes accessed | tf_op | source)
XLA Modules:
  0.0 504.2 jit_solution(5875159322749325888)
XLA Ops:
  7.2 0.7 all-gather.4.cloned.1.call-update
  7.9 0.7 all-gather.6.cloned.1.call-update
  8.7 0.7 all-gather.8.cloned.1.call-update
  9.4 0.7 compare_reduce_fusion
  10.1 0.7 select_reduce_fusion.1
  10.9 0.7 and_select_fusion
  11.6 48.0 %all-gather.4.cloned.1.call-done = bf16[512,2048]{1,0:T(8,128)(2,1)} async-done(((bf16[512,256]{1,0:T(8,128)(2,1)}), bf16[512,2048]{1,0:T(8,128)(2,1)}) %all-gather.4.cloned.1.call-update) | async-done | bytes 2097168 | tf_op jit(solution)/shard_map/all_gather | solution.py:29
  59.6 52.6 %all-gather.6.cloned.1.call-done = bf16[1,2048,1024]{2,1,0:T(8,128)(2,1)} async-done(((bf16[1,64,1024]{2,1,0:T(8,128)(2,1)}), bf16[1,2048,1024]{2,1,0:T(8,128)(2,1)}) %all-gather.6.cloned.1.call-update) | async-done | bytes 4194320 | tf_op jit(solution)/shard_map/all_gather | solution.py:31
  112.2 5.2 %multiply_reduce_fusion.1 = (f32[512]{0:T(512)S(1)}, f32[512,1024]{1,0:T(8,128)S(1)}) fusion(bf16[512,2048]{1,0:T(8,128)(2,1)} %all-gather.4.cloned.1.call-done, bf16[1,2048,1024]{2,1,0:T(8,128)(2,1)} %all-gather.6.cloned.1.call-done), kind=kOutput, calls=%fused_computation.17 | convolution fusion | flops 2148531712 | bytes 8390656 | tf_op jit(solution)/shard_map/dot_general | solution.py:36
  117.4 47.9 %all-gather.8.cloned.1.call-done = bf16[1,2048,1024]{2,1,0:T(8,128)(2,1)} async-done(((bf16[1,64,1024]{2,1,0:T(8,128)(2,1)}), bf16[1,2048,1024]{2,1,0:T(8,128)(2,1)}) %all-gather.8.cloned.1.call-update) | async-done | bytes 4194320 | tf_op jit(solution)/shard_map/all_gather | solution.py:32
  165.3 4.7 fusion.16
  170.0 2.0 copy-done
  171.9 1.1 fusion.8
  173.1 0.6 convert_reduce_fusion
  173.7 51.4 %psum.14 = f32[]{:T(128)} all-reduce(f32[]{:T(128)} %get-tuple-element.18), channel_id=1, replica_groups=mesh['seq'=32,'cb'=8] {'seq'}, use_global_device_ids=true, to_apply=%region_7.8 | all-reduce | flops 1 | bytes 8 | tf_op jit(solution)/shard_map/psum | solution.py:50
  225.8 3.5 multiply_convert_fusion
  229.3 2.4 multiply_reduce_fusion
  231.8 0.4 multiply_convert_fusion.1
  232.2 1.2 copy-done.4
  233.4 4.4 convert_bitcast_fusion
  237.8 6.4 %copy.13 = bf16[2048,1024]{1,0:T(8,128)(2,1)} copy(bf16[2048,1024]{0,1:T(8,128)(2,1)} %convert_bitcast_fusion) | data formatting | bytes 8388608
  244.2 0.2 reduce-scatter.8.cloned.1.call-start
  244.4 6.0 %convolution_convert_fusion = bf16[2048,1024]{1,0:T(8,128)(2,1)} fusion(bf16[512,2048]{1,0:T(8,128)(2,1)} %copy-done.1, f32[512,1024]{1,0:T(8,128)S(1)} %get-tuple-element.21, f32[512]{0:T(512)S(1)} %add_rsqrt_fusion), kind=kOutput, calls=%fused_computation.13 | convolution fusion | flops 2150629376 | bytes 8390656 | tf_op jit(solution)/shard_map/dot_general | solution.py:62
  250.5 0.0 reduce-scatter.6.cloned.1.call-start
  250.5 6.5 %fusion.4 = f32[512,2048]{1,0:T(8,128)} fusion(bf16[512,1024]{1,0:T(8,128)(2,1)S(1)} %multiply_convert_fusion.1, bf16[1,2048,1024]{2,1,0:T(8,128)(2,1)} %all-gather.6.cloned.1.call-done), kind=kOutput, calls=%fused_computation.4 | convolution fusion | flops 2147483648 | bytes 9437184 | tf_op jit(solution)/shard_map/dot_general | solution.py:76
  258.4 88.3 %psum.15 = f32[]{:T(128)} all-reduce(f32[]{:T(128)S(6)} %div.35), channel_id=1, replica_groups=mesh['seq'=32,'cb'=8] {'seq','cb'}, use_global_device_ids=true, to_apply=%region_8.9 | all-reduce | flops 1 | bytes 8 | tf_op jit(solution)/shard_map/psum | solution.py:51
  346.7 1.1 copy.14
  347.8 0.9 copy.12
  348.7 89.4 %reduce-scatter.8.cloned.1.call-done = bf16[64,1024]{1,0:T(8,128)(2,1)} async-done(((bf16[2048,1024]{1,0:T(8,128)(2,1)}), bf16[64,1024]{1,0:T(8,128)(2,1)}) %reduce-scatter.8.cloned.1.call-update) | async-done | bytes 131088 | tf_op jit(solution)/shard_map/reduce_scatter | solution.py:69
  438.1 1.6 bitcast_convert_fusion.1
  439.7 55.9 %reduce-scatter.6.cloned.1.call-done = f32[512,256]{1,0:T(8,128)} async-done(((f32[512,2048]{1,0:T(8,128)}), f32[512,256]{1,0:T(8,128)}) %reduce-scatter.6.cloned.1.call-update) | async-done | bytes 524304 | tf_op jit(solution)/shard_map/reduce_scatter | solution.py:79
  495.6 1.8 convert_element_type.34
  (21 shorter events, 0.3 us)
Async XLA Ops:
  7.2 52.5 %all-gather.4.cloned.1.call-start = ((), (), s32[]{:S(2)}) async-start(), calls=%async_computation.3 | async-start | bytes 2359296 | tf_op jit(solution)/shard_map/all_gather | solution.py:29
  7.9 104.3 %all-gather.6.cloned.1.call-start = ((), (), s32[]{:S(2)}) async-start(), calls=%async_computation.4 | async-start | bytes 4325376 | tf_op jit(solution)/shard_map/all_gather | solution.py:31
  8.6 156.7 %all-gather.8.cloned.1.call-start = ((), (), s32[]{:S(2)}) async-start(), calls=%async_computation.5 | async-start | bytes 4325376 | tf_op jit(solution)/shard_map/all_gather | solution.py:32
  9.4 337.3 %reduce-scatter.10.cloned.1.call-start = ((), (), s32[]{:S(2)}) async-start(), calls=%async_computation.8 | async-start | bytes 4325376
  170.0 2.0 copy-start
  170.0 3.1 copy-start.2
  225.7 3.6 copy-start.3
  229.3 2.5 copy-start.1
  231.8 1.6 copy-start.4
  244.2 193.9 %reduce-scatter.8.cloned.1.call-start = ((), (), s32[]{:S(2)}) async-start(), calls=%async_computation.7 | async-start | bytes 4325376 | tf_op jit(solution)/shard_map/reduce_scatter | solution.py:69
  250.5 245.1 %reduce-scatter.6.cloned.1.call-start = ((), (), s32[]{:S(2)}) async-start(), calls=%async_computation.6 | async-start | bytes 4718592 | tf_op jit(solution)/shard_map/reduce_scatter | solution.py:79
Sparse Core Ops, SparseCore 0:
  9.7 49.8 all-gather.3
  62.2 49.9 all-gather.5
  114.8 50.5 all-gather.7
  244.3 100.4 reduce-scatter.9
  349.1 88.9 reduce-scatter.7
  440.5 55.0 reduce-scatter.5
where the time goes:
time: 506 us; the launch traced here: 504 us
  waiting for transfers between devices  296 us (58%)
  blocking collectives  140 us (28%)
  matrix products  29.2 us (6%)
  between operations  16.3 us (3%)
  local copies, waits for them, and re-layouts  11.5 us (2%)
  other arithmetic  11.3 us (2%)
    reduce_scatter x1, waiting for transfers between devices, local(): lax.psum_scatter(head_term.astype(jnp.bfloat16), 'seq', scatter_dimension...  89.4 us
    psum x1, blocking collectives, local(): loss = lax.psum(jnp.sum(entropy_terms) / count / cb_total, ('seq', 'cb'))  88.3 us
    reduce_scatter x1, waiting for transfers between devices, local(): lax.psum_scatter(context_term, 'cb', scatter_dimension=1, tiled=True)  55.9 us
    all_gather x1, waiting for transfers between devices, local(): lax.all_gather(w_in, 'seq', axis=1, tiled=True)  52.6 us
    psum x1, blocking collectives, local(): count = lax.psum(jnp.sum(keep_float), 'seq')  51.4 us
    all_gather x1, waiting for transfers between devices, local(): full_rows = lax.all_gather(context, 'cb', axis=1, tiled=True)  48 us
    all_gather x1, waiting for transfers between devices, local(): lax.all_gather(w_head, 'seq', axis=1, tiled=True)  47.9 us
    unnamed x13, local copies, waits for them, and re-layouts  11.5 us
  transfers between devices with their start and end apart: 6, of which 5 were waited for; matrix products, arithmetic and copies ran while one was open for 5% of the time, Pallas kernels for 0%

commit v1 on v0

v1 whole, which is shorter than its diff:
```python
import jax
import jax.numpy as jnp
from jax import lax
from jax.experimental import pallas as pl
from jax.experimental.pallas import tpu as pltpu
from jax.sharding import PartitionSpec as P

FRAMES = 256
EPS = 1e-06
BF = jnp.bfloat16
F32 = jnp.float32
NX, NY, NC, NZ = 4, 4, 2, 8
TILE = 256
VMEM_LIMIT = 50 * 1024 * 1024


def seq_index(x, y, c):
    return (x * NY + y) * NC + c


def moves(step):
    pairs = []
    for x in range(NX):
        for y in range(NY):
            for c in range(NC):
                to_x, to_y, to_c = step(x, y, c)
                pairs.append((seq_index(x, y, c), seq_index(to_x % NX, to_y % NY, to_c)))
    return pairs


def shift_x(k):
    return moves(lambda x, y, c: (x + k, y, c))


def shift_y(k):
    return moves(lambda x, y, c: (x, y + k, c))


def lane_x(k):
    return moves(lambda x, y, c: (x + k * (1 - 2 * c), y, c))


def lane_y(k):
    return moves(lambda x, y, c: (x, y + k * (1 - 2 * c), c))


def swap_core():
    return moves(lambda x, y, c: (x, y, 1 - c))


def shift_z(k):
    return [(i, (i + k) % NZ) for i in range(NZ)]


def lookup(table, index):
    spots = jnp.arange(table.shape[0], dtype=jnp.int32)
    return jnp.sum(jnp.where(index[:, None] == spots[None, :], table[None, :], 0), axis=1)


def together(*values):
    return lax.optimization_barrier(values)


def gather_z(block):
    z = lax.axis_index("cb")
    width = block.shape[1]
    full = jnp.zeros((block.shape[0], NZ * width), block.dtype)
    full = lax.dynamic_update_slice(full, block, (0, z * width))
    for k in (4, 3, -3, 2, -2, 1, -1):
        piece = lax.ppermute(block, "cb", shift_z(k))
        full = lax.dynamic_update_slice(full, piece, (0, ((z - k) % NZ) * width))
    return full


def dot(a, b, dims):
    return lax.dot_general(a, b, (dims, ((), ())), preferred_element_type=F32)


def forward_body(
    core, rows, labels, weight, keeps, pair, pair_blocks,
    normed, normed_bf, inverse, grad_keep, grad_send, entropy,
    w_in, w_head, logits, sems,
):
    c = core[0]
    n_rows, width = normed.shape
    vocab = logits.shape[1]
    half = vocab // 2
    load_in = pltpu.make_async_copy(pair.at[:, pl.ds(0, width)], w_in, sems.at[0])
    load_in.start()
    loads = []
    for part in range(NC):
        parity = jnp.bitwise_xor(c, part)
        for y in range(NY):
            copy = pltpu.make_async_copy(
                pair_blocks.at[:, y, parity, :, pl.ds(width, width)],
                w_head.at[part, y],
                sems.at[1 + part * NY + y],
            )
            copy.start()
            loads.append(copy)
    load_in.wait()

    def hidden_tile(n, squares):
        cols = pl.ds(pl.multiple_of(n * TILE, TILE), TILE)
        tile = dot(rows[...], w_in[:, cols], ((1,), (0,)))
        normed[:, cols] = tile
        return squares + jnp.sum(tile * tile, axis=1, keepdims=True)

    squares = lax.fori_loop(0, width // TILE, hidden_tile, jnp.zeros((n_rows, 1), F32))
    inv = lax.rsqrt(squares / width + EPS)
    inverse[...] = inv
    for n in range(width // TILE):
        cols = pl.ds(n * TILE, TILE)
        tile = normed[:, cols] * inv
        normed[:, cols] = tile
        normed_bf[:, cols] = tile.astype(BF)
    for copy in loads:
        copy.wait()

    def logits_tile(n, peak):
        part, y = n // NY, n % NY
        block = w_head[part, y].reshape(TILE, width)
        tile = dot(normed_bf[...], block, ((1,), (1,)))
        logits[:, pl.ds(pl.multiple_of(n * TILE, TILE), TILE)] = tile
        return jnp.maximum(peak, jnp.max(tile, axis=1, keepdims=True))

    tiles = vocab // TILE
    peak = lax.fori_loop(0, tiles, logits_tile, jnp.full((n_rows, 1), -jnp.inf, F32))
    label = labels[...]
    spots = lax.broadcasted_iota(jnp.int32, (n_rows, TILE), 1)

    def exp_tile(n, carry):
        total, picked = carry
        cols = pl.ds(pl.multiple_of(n * TILE, TILE), TILE)
        tile = logits[:, cols]
        picked = picked + jnp.sum(
            jnp.where(spots == label - n * TILE, tile, 0.0), axis=1, keepdims=True
        )
        tile = jnp.exp(tile - peak)
        logits[:, cols] = tile
        return total + jnp.sum(tile, axis=1, keepdims=True), picked

    zero = jnp.zeros((n_rows, 1), F32)
    total, picked = lax.fori_loop(0, tiles, exp_tile, (zero, zero))
    entropy[...] = jnp.where(keeps[...] > 0, peak + jnp.log(total) - picked, 0.0)
    scale = weight[...] / total
    flat = weight[...]

    def grad_tile(n, out, offset):
        cols = pl.ds(pl.multiple_of(n * TILE, TILE), TILE)
        from_cols = pl.ds(pl.multiple_of(n * TILE + offset, TILE), TILE)
        hit = spots == label - (n * TILE + offset)
        out[:, cols] = (logits[:, from_cols] * scale - jnp.where(hit, flat, 0.0)).astype(BF)

    def keep_tile(n, _):
        grad_tile(n, grad_keep, 0)
        return _

    def send_tile(n, _):
        grad_tile(n, grad_send, half)
        return _

    lax.fori_loop(0, half // TILE, keep_tile, 0)
    lax.fori_loop(0, half // TILE, send_tile, 0)


def forward(core, rows, labels, weight, keeps, pair):
    n_rows = rows.shape[0]
    deep, both = pair.shape
    width = both // 2
    vocab = deep
    block_rows = deep // (NX * NY * NC)
    whole = pl.BlockSpec(memory_space=pltpu.VMEM)
    return pl.pallas_call(
        forward_body,
        out_shape=[
            jax.ShapeDtypeStruct((n_rows, width), F32),
            jax.ShapeDtypeStruct((n_rows, width), BF),
            jax.ShapeDtypeStruct((n_rows, 1), F32),
            jax.ShapeDtypeStruct((n_rows, vocab // 2), BF),
            jax.ShapeDtypeStruct((n_rows, vocab // 2), BF),
            jax.ShapeDtypeStruct((n_rows, 1), F32),
        ],
        in_specs=[pl.BlockSpec(memory_space=pltpu.SMEM)] + [whole] * 4
        + [pl.BlockSpec(memory_space=pl.ANY)] * 2,
        out_specs=[whole] * 6,
        scratch_shapes=[
            pltpu.VMEM((deep, width), BF),
            pltpu.VMEM((NC, NY, NX, block_rows, width), BF),
            pltpu.VMEM((n_rows, vocab), F32),
            pltpu.SemaphoreType.DMA((1 + NC * NY,)),
        ],
        compiler_params=pltpu.CompilerParams(vmem_limit_bytes=VMEM_LIMIT),
        cost_estimate=pl.CostEstimate(
            flops=4 * n_rows * deep * width, bytes_accessed=16 << 20, transcendentals=n_rows * vocab
        ),
        name="forward_rows",
    )(core, rows, labels, weight, keeps, pair, pair.reshape(NX, NY, NC, block_rows, both))


def hidden_grad_body(
    core, grad_keep, grad_send, normed, inverse, pair_blocks, out, w_head, grad, sems
):
    c = core[0]
    n_rows, width = normed.shape
    half = grad_keep.shape[1]
    loads = []
    for part in range(NC):
        parity = jnp.bitwise_xor(c, part)
        for y in range(NY):
            copy = pltpu.make_async_copy(
                pair_blocks.at[:, y, parity, :, pl.ds(width, width)],
                w_head.at[part, y],
                sems.at[part * NY + y],
            )
            copy.start()
            loads.append(copy)
    for copy in loads:
        copy.wait()

    def grad_tile(n, mean):
        cols = pl.ds(pl.multiple_of(n * TILE, TILE), TILE)
        tile = dot(grad_keep[...], w_head[0, :, :, :, cols].reshape(half, TILE), ((1,), (0,)))
        tile += dot(grad_send[...], w_head[1, :, :, :, cols].reshape(half, TILE), ((1,), (0,)))
        grad[:, cols] = tile
        return mean + jnp.sum(tile * normed[:, cols], axis=1, keepdims=True)

    mean = lax.fori_loop(0, width // TILE, grad_tile, jnp.zeros((n_rows, 1), F32)) / width
    inv = inverse[...]
    for n in range(width // TILE):
        cols = pl.ds(n * TILE, TILE)
        out[:, cols] = (inv * (grad[:, cols] - normed[:, cols] * mean)).astype(BF)


def hidden_grad(core, grad_keep, grad_send, normed, inverse, pair):
    n_rows, width = normed.shape
    deep, both = pair.shape
    block_rows = deep // (NX * NY * NC)
    whole = pl.BlockSpec(memory_space=pltpu.VMEM)
    return pl.pallas_call(
        hidden_grad_body,
        out_shape=jax.ShapeDtypeStruct((n_rows, width), BF),
        in_specs=[pl.BlockSpec(memory_space=pltpu.SMEM)] + [whole] * 4
        + [pl.BlockSpec(memory_space=pl.ANY)],
        out_specs=whole,
        scratch_shapes=[
            pltpu.VMEM((NC, NY, NX, block_rows, width), BF),
            pltpu.VMEM((n_rows, width), F32),
            pltpu.SemaphoreType.DMA((NC * NY,)),
        ],
        compiler_params=pltpu.CompilerParams(vmem_limit_bytes=VMEM_LIMIT),
        cost_estimate=pl.CostEstimate(
            flops=2 * n_rows * deep * width, bytes_accessed=10 << 20, transcendentals=0
        ),
        name="hidden_grad",
    )(core, grad_keep, grad_send, normed, inverse, pair.reshape(NX, NY, NC, block_rows, both))


def weight_grad_body(order, a_here, a_there, b_here, b_there, *rest):
    outs, (turned_here, turned_there) = rest[:4], rest[4:]
    block = outs[0].shape[0]
    width = b_here.shape[1]
    for j in range(4):
        cols = pl.ds(pl.multiple_of(order[j] * block, block), block)
        turned_here[j * block : (j + 1) * block, :] = a_here[:, cols].T
        turned_there[j * block : (j + 1) * block, :] = a_there[:, cols].T

    def tile_step(n, _):
        cols = pl.ds(pl.multiple_of(n * TILE, TILE), TILE)
        tile = dot(turned_here[...], b_here[:, cols], ((1,), (0,)))
        tile += dot(turned_there[...], b_there[:, cols], ((1,), (0,)))
        for j in range(4):
            outs[j][:, cols] = tile[j * block : (j + 1) * block].astype(outs[j].dtype)
        return _

    lax.fori_loop(0, width // TILE, tile_step, 0)


def weight_grad(order, a_here, a_there, b_here, b_there):
    n_rows, deep = a_here.shape
    width = b_here.shape[1]
    block = deep // 4
    whole = pl.BlockSpec(memory_space=pltpu.VMEM)
    return pl.pallas_call(
        weight_grad_body,
        out_shape=[jax.ShapeDtypeStruct((block, width), t) for t in (BF, BF, F32, F32)],
        in_specs=[pl.BlockSpec(memory_space=pltpu.SMEM)] + [whole] * 4,
        out_specs=[whole] * 4,
        scratch_shapes=[pltpu.VMEM((deep, n_rows), BF)] * 2,
        compiler_params=pltpu.CompilerParams(vmem_limit_bytes=VMEM_LIMIT),
        cost_estimate=pl.CostEstimate(
            flops=4 * n_rows * deep * width, bytes_accessed=8 << 20, transcendentals=0
        ),
        name="weight_grad",
    )(order, a_here, a_there, b_here, b_there)


def send_order(here, c, count):
    way = 1 - 2 * c
    return jnp.stack(
        [(here + 2) % count, (here - way) % count, (here + way) % count, here]
    ).astype(jnp.int32)


def first_stage(blocks, lane):
    relay, against, along, mine = blocks
    passing = lax.ppermute(relay, "seq", lane(1))
    direct = lax.ppermute(against, "seq", lane(-1))
    merged = (along + passing.astype(F32)).astype(BF)
    last = lax.ppermute(merged, "seq", lane(1))
    return mine + direct.astype(F32) + last.astype(F32)


def second_stage(part, here, count, shift):
    width = part.shape[1]
    blocks = part.reshape(count, -1, width)
    total = lax.dynamic_index_in_dim(blocks, here, 0, keepdims=False)
    small = blocks.astype(BF)
    for k in (2, 1, 3):
        piece = lax.dynamic_index_in_dim(small, (here + k) % count, 0, keepdims=False)
        total = total + lax.ppermute(piece, "seq", shift(k)).astype(F32)
    return total


def local(context, lengths, tokens, masks, w_in, w_head):
    seq_count = lax.axis_size("seq")
    cb_total = lax.axis_size("cb") * w_in.shape[0]
    seq_here = lax.axis_index("seq")
    c, y, x = seq_here % NC, (seq_here // NC) % NY, seq_here // (NC * NY)
    core = jnp.reshape(c, (1,)).astype(jnp.int32)
    rows_here, slab = context.shape
    streams_here = rows_here // FRAMES
    w_rows, width = w_in.shape[1:]
    vocab = w_rows * seq_count
    pair = lax.all_gather(jnp.concatenate([w_in[0], w_head[0]], axis=1), "seq", axis=0, tiled=True)

    positions = jnp.arange(rows_here, dtype=jnp.int32)
    own_stream = seq_here * streams_here + positions // FRAMES
    live = positions % FRAMES < lookup(lengths, own_stream)
    keeps = live & (masks[:, 0] > 0)
    keep_float = keeps.astype(F32)
    token = tokens[:, 0]
    owner, spot = token // w_rows, token % w_rows
    own_x, own_y, own_c = owner // (NY * NC), (owner // NC) % NY, owner % NC
    column = ((((own_c + c) % NC) * NY + own_y) * NX + own_x) * w_rows + spot
    labels = jnp.where(keeps, column, -1)
    tally = jnp.concatenate([keep_float, jnp.zeros((1024 - rows_here,), F32)]).reshape(8, 128)
    count = jnp.sum(lax.all_gather(tally, "seq", axis=0))
    rows_total = FRAMES * streams_here * seq_count
    weight = keep_float * (rows_total / (count * cb_total))

    full_rows = gather_z(context)
    by_core = full_rows.reshape(rows_here, NX * NY, NC, w_rows)
    even = by_core[:, :, 0].reshape(rows_here, -1)
    odd = by_core[:, :, 1].reshape(rows_here, -1)
    rows_keep = jnp.where(c == 0, even, odd)
    rows_other = lax.ppermute(jnp.where(c == 0, odd, even), "seq", swap_core())
    full_rows, weight, rows_keep, rows_other, pair = together(
        full_rows, weight, rows_keep, rows_other, pair
    )

    normed, normed_bf, inverse, grad_keep, grad_send, entropy = forward(
        core, full_rows, labels[:, None], weight[:, None], keep_float[:, None], pair
    )
    grad_other = lax.ppermute(grad_send, "seq", swap_core())
    normed_other = lax.ppermute(normed_bf, "seq", swap_core())
    tile = jnp.full((8, 128), jnp.sum(entropy) / count / cb_total, F32)
    tile_in = lax.ppermute(tile, "seq", swap_core())
    grad_hidden = hidden_grad(core, grad_keep, grad_send, normed, inverse, pair)
    grad_hidden, tile, tile_in = together(grad_hidden, tile, tile_in)
    hidden_other = lax.ppermute(grad_hidden, "seq", swap_core())
    tile = tile + tile_in
    tile_in = lax.ppermute(tile, "cb", shift_z(1))
    context_term = dot(grad_hidden, pair[:, :width], ((1,), (1,))).astype(BF)
    grad_other, normed_other, context_term, tile, tile_in = together(
        grad_other, normed_other, context_term, tile, tile_in
    )
    context_part = lax.psum_scatter(context_term, "cb", scatter_dimension=1, tiled=True)
    tile = tile + tile_in
    tile_in = lax.ppermute(tile, "cb", shift_z(2))
    head_blocks = weight_grad(send_order(y, c, NY), grad_keep, grad_other, normed_bf, normed_other)
    head_blocks, hidden_other, tile, tile_in = together(head_blocks, hidden_other, tile, tile_in)
    tile = tile + tile_in
    tile_in = lax.ppermute(tile, "cb", shift_z(4))
    head_sum = first_stage(head_blocks, lane_y)
    in_blocks = weight_grad(send_order(x, c, NX), rows_keep, rows_other, grad_hidden, hidden_other)
    in_blocks, tile, tile_in = together(in_blocks, tile, tile_in)
    in_sum = first_stage(in_blocks, lane_x)
    tile = tile + tile_in
    tile = tile + lax.ppermute(tile, "seq", shift_x(1))
    tile = tile + lax.ppermute(tile, "seq", shift_x(2))
    tile = tile + lax.ppermute(tile, "seq", shift_y(1))
    tile = tile + lax.ppermute(tile, "seq", shift_y(2))
    head_part = second_stage(head_sum, x, NX, shift_x)
    in_part = second_stage(in_sum, y, NY, shift_y)
    return (tile[0, 0], context_part, in_part[None], head_part[None])


def solution(mesh):
    in_specs = (
        P("seq", "cb"),
        P(),
        P("seq", "cb"),
        P("seq", "cb"),
        P("cb", "seq", None),
        P("cb", "seq", None),
    )
    out_specs = (P(), P("seq", "cb"), P("cb", "seq", None), P("cb", "seq", None))
    return jax.shard_map(local, mesh=mesh, in_specs=in_specs, out_specs=out_specs, check_vma=False)
```

time: 506 us -> 217 us (0.43)
  waiting for transfers between devices: 296 us -> 62.7 us
  blocking collectives: 140 us -> 24.5 us
  starting transfers between devices: 0.42 us -> 43.1 us
  Pallas kernels: 0 us -> 39.8 us
  matrix products: 29.2 us -> 3.74 us
    all_gather x3 -> x1, waiting for transfers between devices: 148 us -> 0.02 us  [local(): lax.all_gather(jnp.concatenate([w_in[0], w_head[0]], axis=1), 'seq', axis...]
    psum x2 -> x0, blocking collectives: 140 us -> none  [the longest x1 88.3 us: local(): loss = lax.psum(jnp.sum(entropy_terms) / count / cb_total, ('seq', 'cb'))]
    reduce_scatter x1 -> x0, waiting for transfers between devices: 89.4 us -> none  [local(): lax.psum_scatter(head_term.astype(jnp.bfloat16), 'seq', scatter_dimension...]
    ppermute x0 -> x31, waiting for transfers between devices: none -> 62.6 us  [the longest x7 31.4 us: gather_z(): piece = lax.ppermute(block, 'cb', shift_z(k))]
    reduce_scatter x1, waiting for transfers between devices: 55.9 us -> 0.01 us  [local(): lax.psum_scatter(context_term, 'cb', scatter_dimension=1, tiled=True)]
    ppermute x0 -> x31, starting transfers between devices: none -> 43 us  [the longest x7 16.5 us: gather_z(): piece = lax.ppermute(block, 'cb', shift_z(k))]
    pallas_call x0 -> x4, Pallas kernels: none -> 39.8 us  [the longest x1 19.2 us: forward(): pl.pallas_call(forward_body, out_shape=[jax.ShapeDtypeStruct((n_rows, wid...]
    dot_general x6 -> x1, matrix products: 29.2 us -> 3.74 us  [dot(): return lax.dot_general(a, b, (dims, ((), ())), preferred_element_type=F32)]
  transfers between devices with their start and end apart: 6 -> 33, of which waited for: 5 -> 14; matrix products, arithmetic and copies ran while one was open for 5% -> 12% of each run, Pallas kernels for 0% -> 9%
where the time goes in v1:
time: 217 us
  waiting for transfers between devices  62.7 us (29%)
  starting transfers between devices  43.1 us (20%)
  Pallas kernels  39.8 us (18%)
  blocking collectives  24.5 us (11%)
  between operations  16.8 us (8%)
  other arithmetic  14.1 us (6%)
  local copies, waits for them, and re-layouts  12.4 us (6%)
  matrix products  3.74 us (2%)
    ppermute x7, waiting for transfers between devices, gather_z(): piece = lax.ppermute(block, 'cb', shift_z(k))  31.4 us
    all_gather x1, blocking collectives, local(): count = jnp.sum(lax.all_gather(tally, 'seq', axis=0))  24.5 us
    pallas_call x1, Pallas kernels, forward(): pl.pallas_call(forward_body, out_shape=[jax.ShapeDtypeStruct((n_rows, wid...  19.2 us
    ppermute x7, starting transfers between devices, gather_z(): piece = lax.ppermute(block, 'cb', shift_z(k))  16.5 us
    pallas_call x2, Pallas kernels, weight_grad(): pl.pallas_call(weight_grad_body, out_shape=[jax.ShapeDtypeStruct((block,...  12.8 us
    ppermute x1, waiting for transfers between devices, local(): tile = tile + lax.ppermute(tile, 'seq', shift_x(1))  9.25 us
    ppermute x6, starting transfers between devices, second_stage(): total = total + lax.ppermute(piece, 'seq', shift(k)).astype(F32)  8.37 us
    pallas_call x1, Pallas kernels, hidden_grad(): pl.pallas_call(hidden_grad_body, out_shape=jax.ShapeDtypeStruct((n_rows,...  7.8 us
  transfers between devices with their start and end apart: 33, of which 14 were waited for; matrix products, arithmetic and copies ran while one was open for 12% of the time, Pallas kernels for 9%

profile of v1, /device:TPU:24, one launch (start us, length us, event | category | flops | bytes accessed | tf_op | source)
XLA Modules:
  0.0 217.0 jit_solution(9447284593231842254)
XLA Ops:
  7.3 1.7 pad_maximum_fusion
  9.1 7.3 %collective-permute-start = (bf16[512,256]{1,0:T(8,128)(2,1)}, bf16[512,256]{1,0:T(8,128)(2,1)}, u32[]{:S(2)}, u32[]{:S(2)}) collective-permute-start(bf16[512,256]{1,0:T(8,128)(2,1)} %param.6), channel_id=1, source_target_pairs={{0,4},{1,5},{2,6},{3,7},{4,0},{5,1},{6,2},{7,3},{8,12},{9,13},{10,... | collective-permute-start | bytes 786440 | tf_op jit(solution)/shard_map/ppermute | solution.py:70
  16.3 1.9 collective-permute-start.1
  18.3 3.1 %collective-permute-start.2 = (bf16[512,256]{1,0:T(8,128)(2,1)}, bf16[512,256]{1,0:T(8,128)(2,1)}, u32[]{:S(2)}, u32[]{:S(2)}) collective-permute-start(bf16[512,256]{1,0:T(8,128)(2,1)} %param.6), channel_id=1, source_target_pairs={{0,5},{1,6},{2,7},{3,0},{4,1},{5,2},{6,3},{7,4},{8,13},{9,14},{10,... | collective-permute-start | bytes 786440 | tf_op jit(solution)/shard_map/ppermute | solution.py:70
  22.8 2.7 %collective-permute-start.4 = (bf16[512,256]{1,0:T(8,128)(2,1)}, bf16[512,256]{1,0:T(8,128)(2,1)S(1)}, u32[]{:S(2)}, u32[]{:S(2)}) collective-permute-start(bf16[512,256]{1,0:T(8,128)(2,1)} %param.6), channel_id=1, source_target_pairs={{0,6},{1,7},{2,0},{3,1},{4,2},{5,3},{6,4},{7,5},{8,14},{9,15},{10,... | collective-permute-start | bytes 786440 | tf_op jit(solution)/shard_map/ppermute | solution.py:70
  27.5 5.7 %collective-permute-done = bf16[512,256]{1,0:T(8,128)(2,1)} collective-permute-done((bf16[512,256]{1,0:T(8,128)(2,1)}, bf16[512,256]{1,0:T(8,128)(2,1)}, u32[]{:S(2)}, u32[]{:S(2)}) %collective-permute-start) | collective-permute-done | bytes 262176 | tf_op jit(solution)/shard_map/ppermute | solution.py:70
  34.1 15.5 %collective-permute-done.1 = bf16[512,256]{1,0:T(8,128)(2,1)} collective-permute-done((bf16[512,256]{1,0:T(8,128)(2,1)}, bf16[512,256]{1,0:T(8,128)(2,1)}, u32[]{:S(2)}, u32[]{:S(2)}) %collective-permute-start.1) | collective-permute-done | bytes 262176 | tf_op jit(solution)/shard_map/ppermute | solution.py:70
  51.7 5.1 %collective-permute-done.3 = bf16[512,256]{1,0:T(8,128)(2,1)} collective-permute-done((bf16[512,256]{1,0:T(8,128)(2,1)}, bf16[512,256]{1,0:T(8,128)(2,1)}, u32[]{:S(2)}, u32[]{:S(2)}) %collective-permute-start.3) | collective-permute-done | bytes 262176 | tf_op jit(solution)/shard_map/ppermute | solution.py:70
  57.8 3.7 %collective-permute-done.5 = bf16[512,256]{1,0:T(8,128)(2,1)S(1)} collective-permute-done((bf16[512,256]{1,0:T(8,128)(2,1)S(1)}, bf16[512,256]{1,0:T(8,128)(2,1)S(1)}, u32[]{:S(2)}, u32[]{:S(2)}) %collective-permute-start.5) | collective-permute-done | bytes 262176 | tf_op jit(solution)/shard_map/ppermute | solution.py:70
  63.0 2.7 %copy.47 = bf16[512,2048]{0,1:T(8,128)(2,1)} copy(bf16[512,2048]{1,0:T(8,128)(2,1)S(1)} %constant_dynamic-update-slice_fusion.rows) | data formatting | bytes 4194304 | tf_op jit(solution)/shard_map/dynamic_update_slice | solution.py:71
  65.7 2.7 %broadcast_select_fusion = (bf16[512,16,1,64]{0,3,2,1:T(8,128)(2,1)S(1)}, bf16[512,16,1,64]{0,3,2,1:T(8,128)(2,1)}) fusion(pred[]{:T(512)S(6)} %eq.48, bf16[512,16,2,64]{0,3,2,1:T(8,128)(2,1)} %bitcast.57), kind=kLoop, calls=%fused_computation.7 | loop fusion | flops 1048576 | bytes 4194305 | tf_op jit(solution)/shard_map/jit(_where)/select_n | solution.py:357
  69.2 24.5 %all_gather.6 = f32[32,8,128]{2,1,0:T(8,128)S(1)} all-gather(f32[1,8,128]{2,1,0:T(8,128)S(1)} %convert_bitcast_fusion), channel_id=1, replica_groups=mesh['seq'=32,'cb'=8] {'seq'}, dimensions={0}, use_global_device_ids=true | all-gather | bytes 135168 | tf_op jit(solution)/shard_map/all_gather | solution.py:348
  96.2 19.2 %forward_rows.1 = (f32[512,1024]{1,0:T(8,128)}, bf16[512,1024]{1,0:T(8,128)(2,1)}, f32[512,1]{1,0:T(8,128)S(1)}, bf16[512,1024]{1,0:T(8,128)(2,1)S(1)}, bf16[512,1024]{1,0:T(8,128)(2,1)}, /*index=5*/f32[512,1]{1,0:T(8,128)S(1)}) custom-call(s32[1]{0:T(128)} %bitcast.10.core, bf16[512,2048]{1,0:T(8,128)(2,1)} %copy-done.4, s32[512,1]{1,0:T(8,128)S(1)} %fusion.14.labels, ...), custom_call_target="tpu_custom_call" | custom-call | flops 4294967296 | bytes 16777216 | tf_op jit(solution)/shard_map/forward_rows/pallas_call | solution.py:174
  119.6 7.8 %hidden_grad.1.b_here = bf16[512,1024]{1,0:T(8,128)(2,1)S(1)} custom-call(s32[1]{0:T(128)} %bitcast.10.core, bf16[512,1024]{1,0:T(8,128)(2,1)S(1)} %get-tuple-element.49.grad_keep.a_here, bf16[512,1024]{1,0:T(8,128)(2,1)S(1)} %copy-done.2, f32[512,1024]{1,0:T(8,128)} %get-tuple-element.51.normed, f32[512,1]{1,0:T(8,128)S(1)} %get-tuple-element.52.inverse, ...), custom_call_target="tpu_custom_call" | custom-call | flops 2147483648 | bytes 10485760 | tf_op jit(solution)/shard_map/hidden_grad/pallas_call | solution.py:240
  127.9 3.7 %fusion.2 = bf16[512,2048]{1,0:T(8,128)(2,1)} fusion(bf16[512,1024]{1,0:T(8,128)(2,1)S(1)} %hidden_grad.1.b_here, bf16[2048,2048]{1,0:T(8,128)(2,1)S(1)} %copy-done.3), kind=kOutput, calls=%fused_computation.2 | convolution fusion | flops 2148532224 | bytes 7340032 | tf_op jit(solution)/shard_map/dot_general | solution.py:76
  132.7 1.7 collective-permute-start.13
  134.4 6.4 %weight_grad.2 = (bf16[256,1024]{1,0:T(8,128)(2,1)}, bf16[256,1024]{1,0:T(8,128)(2,1)}, f32[256,1024]{1,0:T(8,128)S(1)}, f32[256,1024]{1,0:T(8,128)S(1)}) custom-call(s32[4]{0:T(128)S(1)} %pad_add_fusion.1.order, bf16[512,1024]{1,0:T(8,128)(2,1)} %copy-done.1, bf16[512,1024]{1,0:T(8,128)(2,1)} %collective-permute-done.9.a_there, ...), custom_call_target="tpu_custom_call" | custom-call | flops 2147483648 | bytes 8388608 | tf_op jit(solution)/shard_map/weight_grad/pallas_call | solution.py:284
  141.8 2.3 %copy.58.a_here = bf16[512,1024]{1,0:T(8,128)(2,1)} copy(bf16[512,1024]{0,1:T(8,128)(2,1)} %bitcast.62) | data formatting | bytes 2097152 | tf_op jit(solution)/shard_map/optimization_barrier | solution.py:61
  144.1 4.0 %collective-permute-start.14 = (f32[8,128]{1,0:T(8,128)S(1)}, f32[8,128]{1,0:T(8,128)S(1)}, u32[]{:S(2)}, u32[]{:S(2)}) collective-permute-start(f32[8,128]{1,0:T(8,128)S(1)} %add.325), channel_id=1, source_target_pairs={{0,4},{1,5},{2,6},{3,7},{4,0},{5,1},{6,2},{7,3},{8,12},{9,13},{10,... | collective-permute-start | bytes 12296 | tf_op jit(solution)/shard_map/ppermute | solution.py:384
  148.1 6.4 %weight_grad.3 = (bf16[256,1024]{1,0:T(8,128)(2,1)S(1)}, bf16[256,1024]{1,0:T(8,128)(2,1)}, f32[256,1024]{1,0:T(8,128)S(1)}, f32[256,1024]{1,0:T(8,128)S(1)}) custom-call(s32[4]{0:T(128)S(1)} %pad_add_fusion.order, bf16[512,1024]{1,0:T(8,128)(2,1)} %copy.58.a_here, bf16[512,1024]{1,0:T(8,128)(2,1)} %collective-permute-done.7.a_there, ...), custom_call_target="tpu_custom_call" | custom-call | flops 2147483648 | bytes 8388608 | tf_op jit(solution)/shard_map/weight_grad/pallas_call | solution.py:284
  155.8 2.0 add_convert_fusion
  157.8 3.1 %collective-permute-start.27 = (bf16[256,1024]{1,0:T(8,128)(2,1)}, bf16[256,1024]{1,0:T(8,128)(2,1)}, u32[]{:S(2)}, u32[]{:S(2)}) collective-permute-start(bf16[256,1024]{1,0:T(8,128)(2,1)} %add_convert_fusion), channel_id=1, source_target_pairs={{0,16},{8,56},{16,32},{24,8},{32,48},{40,24},{48,0},{56,40},{64,80... | collective-permute-start | bytes 1572872 | tf_op jit(solution)/shard_map/ppermute | solution.py:310
  160.9 2.0 collective-permute-start.19
  162.9 3.9 %collective-permute-done.20 = bf16[256,1024]{1,0:T(8,128)(2,1)S(1)} collective-permute-done((bf16[256,1024]{1,0:T(8,128)(2,1)S(1)}, bf16[256,1024]{1,0:T(8,128)(2,1)S(1)}, u32[]{:S(2)}, u32[]{:S(2)}) %collective-permute-start.20) | collective-permute-done | bytes 524320 | tf_op jit(solution)/shard_map/ppermute | solution.py:307
  169.3 9.2 %collective-permute-done.15 = f32[8,128]{1,0:T(8,128)S(1)} collective-permute-done((f32[8,128]{1,0:T(8,128)S(1)}, f32[8,128]{1,0:T(8,128)S(1)}, u32[]{:S(2)}, u32[]{:S(2)}) %collective-permute-start.15) | collective-permute-done | bytes 4128 | tf_op jit(solution)/shard_map/ppermute | solution.py:390
  178.9 4.8 %collective-permute-done.16 = f32[8,128]{1,0:T(8,128)S(1)} collective-permute-done((f32[8,128]{1,0:T(8,128)S(1)}, f32[8,128]{1,0:T(8,128)S(1)}, u32[]{:S(2)}, u32[]{:S(2)}) %collective-permute-start.16) | collective-permute-done | bytes 4128 | tf_op jit(solution)/shard_map/ppermute | solution.py:391
  183.6 3.6 %collective-permute-done.17 = f32[8,128]{1,0:T(8,128)S(1)} collective-permute-done((f32[8,128]{1,0:T(8,128)S(1)}, f32[8,128]{1,0:T(8,128)S(1)}, u32[]{:S(2)}, u32[]{:S(2)}) %collective-permute-start.17) | collective-permute-done | bytes 4128 | tf_op jit(solution)/shard_map/ppermute | solution.py:392
  188.9 3.5 %collective-permute-done.18 = f32[8,128]{1,0:T(8,128)S(1)} collective-permute-done((f32[8,128]{1,0:T(8,128)S(1)}, f32[8,128]{1,0:T(8,128)S(1)}, u32[]{:S(2)}, u32[]{:S(2)}) %collective-permute-start.18) | collective-permute-done | bytes 4128 | tf_op jit(solution)/shard_map/ppermute | solution.py:393
  194.9 1.8 collective-permute-start.29
  198.5 1.7 collective-permute-start.22
  200.2 3.0 %collective-permute-start.23 = (bf16[64,1024]{1,0:T(8,128)(2,1)S(1)}, bf16[64,1024]{1,0:T(8,128)(2,1)S(1)}, u32[]{:S(2)}, u32[]{:S(2)}) collective-permute-start(bf16[64,1024]{1,0:T(8,128)(2,1)S(1)} %get-tuple-element.94), channel_id=1, source_target_pairs={{0,16},{8,24},{16,32},{24,40},{32,48},{40,56},{48,0},{56,8},{64,80... | collective-permute-start | bytes 393224 | tf_op jit(solution)/shard_map/ppermute | solution.py:321
  205.7 3.7 %collective-permute-done.24 = bf16[64,1024]{1,0:T(8,128)(2,1)S(1)} collective-permute-done((bf16[64,1024]{1,0:T(8,128)(2,1)S(1)}, bf16[64,1024]{1,0:T(8,128)(2,1)S(1)}, u32[]{:S(2)}, u32[]{:S(2)}) %collective-permute-start.24) | collective-permute-done | bytes 131104 | tf_op jit(solution)/shard_map/ppermute | solution.py:321
  (112 shorter events, 29.8 us)
Async XLA Ops:
  7.2 88.8 %all-gather.2.cloned.1.call-start = ((), (), s32[]{:S(2)}) async-start(), calls=%async_computation.1 | async-start | bytes 8650752 | tf_op jit(solution)/shard_map/all_gather | solution.py:335
  9.0 201.2 %reduce-scatter.2.cloned.1.call-start = ((), (), s32[]{:S(2)}) async-start(), calls=%async_computation.2 | async-start | bytes 2359296 | tf_op jit(solution)/shard_map/reduce_scatter | solution.py:378
  9.1 24.1 %collective-permute-start = (bf16[512,256]{1,0:T(8,128)(2,1)}, bf16[512,256]{1,0:T(8,128)(2,1)}, u32[]{:S(2)}, u32[]{:S(2)}) collective-permute-start(bf16[512,256]{1,0:T(8,128)(2,1)} %param.6), channel_id=1, source_target_pairs={{0,4},{1,5},{2,6},{3,7},{4,0},{5,1},{6,2},{7,3},{8,12},{9,13},{10,... | collective-permute-start | bytes 786440 | tf_op jit(solution)/shard_map/ppermute | solution.py:70
  16.3 33.3 %collective-permute-start.1 = (bf16[512,256]{1,0:T(8,128)(2,1)}, bf16[512,256]{1,0:T(8,128)(2,1)}, u32[]{:S(2)}, u32[]{:S(2)}) collective-permute-start(bf16[512,256]{1,0:T(8,128)(2,1)} %param.6), channel_id=1, source_target_pairs={{0,3},{1,4},{2,5},{3,6},{4,7},{5,0},{6,1},{7,2},{8,11},{9,12},{10,... | collective-permute-start | bytes 786440 | tf_op jit(solution)/shard_map/ppermute | solution.py:70
  18.3 32.4 %collective-permute-start.2 = (bf16[512,256]{1,0:T(8,128)(2,1)}, bf16[512,256]{1,0:T(8,128)(2,1)}, u32[]{:S(2)}, u32[]{:S(2)}) collective-permute-start(bf16[512,256]{1,0:T(8,128)(2,1)} %param.6), channel_id=1, source_target_pairs={{0,5},{1,6},{2,7},{3,0},{4,1},{5,2},{6,3},{7,4},{8,13},{9,14},{10,... | collective-permute-start | bytes 786440 | tf_op jit(solution)/shard_map/ppermute | solution.py:70
  21.4 35.4 %collective-permute-start.3 = (bf16[512,256]{1,0:T(8,128)(2,1)}, bf16[512,256]{1,0:T(8,128)(2,1)}, u32[]{:S(2)}, u32[]{:S(2)}) collective-permute-start(bf16[512,256]{1,0:T(8,128)(2,1)} %param.6), channel_id=1, source_target_pairs={{0,2},{1,3},{2,4},{3,5},{4,6},{5,7},{6,0},{7,1},{8,10},{9,11},{10,... | collective-permute-start | bytes 786440 | tf_op jit(solution)/shard_map/ppermute | solution.py:70
  22.8 35.0 %collective-permute-start.4 = (bf16[512,256]{1,0:T(8,128)(2,1)}, bf16[512,256]{1,0:T(8,128)(2,1)S(1)}, u32[]{:S(2)}, u32[]{:S(2)}) collective-permute-start(bf16[512,256]{1,0:T(8,128)(2,1)} %param.6), channel_id=1, source_target_pairs={{0,6},{1,7},{2,0},{3,1},{4,2},{5,3},{6,4},{7,5},{8,14},{9,15},{10,... | collective-permute-start | bytes 786440 | tf_op jit(solution)/shard_map/ppermute | solution.py:70
  33.1 28.4 %collective-permute-start.5 = (bf16[512,256]{1,0:T(8,128)(2,1)S(1)}, bf16[512,256]{1,0:T(8,128)(2,1)S(1)}, u32[]{:S(2)}, u32[]{:S(2)}) collective-permute-start(bf16[512,256]{1,0:T(8,128)(2,1)S(1)} %copy-done.5), channel_id=1, source_target_pairs={{0,1},{1,2},{2,3},{3,4},{4,5},{5,6},{6,7},{7,0},{8,9},{9,10},{10,1... | collective-permute-start | bytes 786440 | tf_op jit(solution)/shard_map/ppermute | solution.py:70
  49.6 13.3 %collective-permute-start.6 = (bf16[512,256]{1,0:T(8,128)(2,1)S(1)}, bf16[512,256]{1,0:T(8,128)(2,1)S(1)}, u32[]{:S(2)}, u32[]{:S(2)}) collective-permute-start(bf16[512,256]{1,0:T(8,128)(2,1)S(1)} %copy-done.5), channel_id=1, source_target_pairs={{0,7},{1,0},{2,1},{3,2},{4,3},{5,4},{6,5},{7,6},{8,15},{9,8},{10,9... | collective-permute-start | bytes 786440 | tf_op jit(solution)/shard_map/ppermute | solution.py:70
  68.9 27.1 %collective-permute-start.7 = (bf16[512,1024]{1,0:T(8,128)(2,1)S(1)}, bf16[512,1024]{1,0:T(8,128)(2,1)}, u32[]{:S(2)}, u32[]{:S(2)}) collective-permute-start(bf16[512,1024]{1,0:T(8,128)(2,1)S(1)} %copy.48), channel_id=1, source_target_pairs={{0,8},{8,0},{16,24},{24,16},{32,40},{40,32},{48,56},{56,48},{64,72... | collective-permute-start | bytes 3145736 | tf_op jit(solution)/shard_map/ppermute | solution.py:357
  115.3 17.0 %collective-permute-start.10 = (bf16[512,1024]{1,0:T(8,128)(2,1)}, bf16[512,1024]{1,0:T(8,128)(2,1)}, u32[]{:S(2)}, u32[]{:S(2)}) collective-permute-start(bf16[512,1024]{1,0:T(8,128)(2,1)} %get-tuple-element.55.b_here), channel_id=1, source_target_pairs={{0,8},{8,0},{16,24},{24,16},{32,40},{40,32},{48,56},{56,48},{64,72... | collective-permute-start | bytes 3145736 | tf_op jit(solution)/shard_map/ppermute | solution.py:366
  115.8 16.6 %collective-permute-start.9 = (bf16[512,1024]{1,0:T(8,128)(2,1)}, bf16[512,1024]{1,0:T(8,128)(2,1)}, u32[]{:S(2)}, u32[]{:S(2)}) collective-permute-start(bf16[512,1024]{1,0:T(8,128)(2,1)} %get-tuple-element.50.grad_send), channel_id=1, source_target_pairs={{0,8},{8,0},{16,24},{24,16},{32,40},{40,32},{48,56},{56,48},{64,72... | collective-permute-start | bytes 3145736 | tf_op jit(solution)/shard_map/ppermute | solution.py:365
  117.9 9.5 %collective-permute-start.8 = (f32[8,128]{1,0:T(8,128)S(1)}, f32[8,128]{1,0:T(8,128)S(1)}, u32[]{:S(2)}, u32[]{:S(2)}) collective-permute-start(f32[8,128]{1,0:T(8,128)S(1)} %broadcast_in_dim.39), channel_id=1, source_target_pairs={{0,8},{8,0},{16,24},{24,16},{32,40},{40,32},{48,56},{56,48},{64,72... | collective-permute-start | bytes 12296 | tf_op jit(solution)/shard_map/ppermute | solution.py:368
  127.5 4.9 %collective-permute-start.11 = (f32[8,128]{1,0:T(8,128)S(1)}, f32[8,128]{1,0:T(8,128)S(1)}, u32[]{:S(2)}, u32[]{:S(2)}) collective-permute-start(f32[8,128]{1,0:T(8,128)S(1)} %add.323), channel_id=1, source_target_pairs={{0,1},{1,2},{2,3},{3,4},{4,5},{5,6},{6,7},{7,0},{8,9},{9,10},{10,1... | collective-permute-start | bytes 12296 | tf_op jit(solution)/shard_map/ppermute | solution.py:373
  132.4 8.4 %collective-permute-start.12 = (bf16[512,1024]{1,0:T(8,128)(2,1)S(1)}, bf16[512,1024]{1,0:T(8,128)(2,1)}, u32[]{:S(2)}, u32[]{:S(2)}) collective-permute-start(bf16[512,1024]{1,0:T(8,128)(2,1)S(1)} %hidden_grad.1.b_here), channel_id=1, source_target_pairs={{0,8},{8,0},{16,24},{24,16},{32,40},{40,32},{48,56},{56,48},{64,72... | collective-permute-start | bytes 3145736 | tf_op jit(solution)/shard_map/ppermute | solution.py:371
  132.7 8.1 %collective-permute-start.13 = (f32[8,128]{1,0:T(8,128)S(1)}, f32[8,128]{1,0:T(8,128)S(1)}, u32[]{:S(2)}, u32[]{:S(2)}) collective-permute-start(f32[8,128]{1,0:T(8,128)S(1)} %add.324), channel_id=1, source_target_pairs={{0,2},{1,3},{2,4},{3,5},{4,6},{5,7},{6,0},{7,1},{8,10},{9,11},{10,... | collective-permute-start | bytes 12296 | tf_op jit(solution)/shard_map/ppermute | solution.py:380
  140.8 15.0 %collective-permute-start.26 = (bf16[256,1024]{1,0:T(8,128)(2,1)}, bf16[256,1024]{1,0:T(8,128)(2,1)}, u32[]{:S(2)}, u32[]{:S(2)}) collective-permute-start(bf16[256,1024]{1,0:T(8,128)(2,1)} %get-tuple-element.83), channel_id=1, source_target_pairs={{0,16},{8,56},{16,32},{24,8},{32,48},{40,24},{48,0},{56,40},{64,80... | collective-permute-start | bytes 1572872 | tf_op jit(solution)/shard_map/ppermute | solution.py:307
  144.1 10.4 %collective-permute-start.14 = (f32[8,128]{1,0:T(8,128)S(1)}, f32[8,128]{1,0:T(8,128)S(1)}, u32[]{:S(2)}, u32[]{:S(2)}) collective-permute-start(f32[8,128]{1,0:T(8,128)S(1)} %add.325), channel_id=1, source_target_pairs={{0,4},{1,5},{2,6},{3,7},{4,0},{5,1},{6,2},{7,3},{8,12},{9,13},{10,... | collective-permute-start | bytes 12296 | tf_op jit(solution)/shard_map/ppermute | solution.py:384
  154.5 12.4 %collective-permute-start.20 = (bf16[256,1024]{1,0:T(8,128)(2,1)S(1)}, bf16[256,1024]{1,0:T(8,128)(2,1)S(1)}, u32[]{:S(2)}, u32[]{:S(2)}) collective-permute-start(bf16[256,1024]{1,0:T(8,128)(2,1)S(1)} %get-tuple-element.79), channel_id=1, source_target_pairs={{0,64},{8,200},{16,80},{24,216},{32,96},{40,232},{48,112},{56,248}... | collective-permute-start | bytes 1572872 | tf_op jit(solution)/shard_map/ppermute | solution.py:307
  155.7 37.2 %collective-permute-start.25 = (bf16[256,1024]{1,0:T(8,128)(2,1)}, bf16[256,1024]{1,0:T(8,128)(2,1)}, u32[]{:S(2)}, u32[]{:S(2)}) collective-permute-start(bf16[256,1024]{1,0:T(8,128)(2,1)} %get-tuple-element.81), channel_id=1, source_target_pairs={{0,48},{8,24},{16,0},{24,40},{32,16},{40,56},{48,32},{56,8},{64,11... | collective-permute-start | bytes 1572872 | tf_op jit(solution)/shard_map/ppermute | solution.py:308
  157.8 35.1 %collective-permute-start.27 = (bf16[256,1024]{1,0:T(8,128)(2,1)}, bf16[256,1024]{1,0:T(8,128)(2,1)}, u32[]{:S(2)}, u32[]{:S(2)}) collective-permute-start(bf16[256,1024]{1,0:T(8,128)(2,1)} %add_convert_fusion), channel_id=1, source_target_pairs={{0,16},{8,56},{16,32},{24,8},{32,48},{40,24},{48,0},{56,40},{64,80... | collective-permute-start | bytes 1572872 | tf_op jit(solution)/shard_map/ppermute | solution.py:310
  160.9 37.2 %collective-permute-start.19 = (bf16[256,1024]{1,0:T(8,128)(2,1)}, bf16[256,1024]{1,0:T(8,128)(2,1)S(1)}, u32[]{:S(2)}, u32[]{:S(2)}) collective-permute-start(bf16[256,1024]{1,0:T(8,128)(2,1)} %get-tuple-element.77), channel_id=1, source_target_pairs={{0,192},{8,72},{16,208},{24,88},{32,224},{40,104},{48,240},{56,120... | collective-permute-start | bytes 1572872 | tf_op jit(solution)/shard_map/ppermute | solution.py:308
  167.8 30.3 %collective-permute-start.21 = (bf16[256,1024]{1,0:T(8,128)(2,1)}, bf16[256,1024]{1,0:T(8,128)(2,1)S(1)}, u32[]{:S(2)}, u32[]{:S(2)}) collective-permute-start(bf16[256,1024]{1,0:T(8,128)(2,1)} %add_convert_fusion.1), channel_id=1, source_target_pairs={{0,64},{8,200},{16,80},{24,216},{32,96},{40,232},{48,112},{56,248}... | collective-permute-start | bytes 1572872 | tf_op jit(solution)/shard_map/ppermute | solution.py:310
  167.9 10.6 %collective-permute-start.15 = (f32[8,128]{1,0:T(8,128)S(1)}, f32[8,128]{1,0:T(8,128)S(1)}, u32[]{:S(2)}, u32[]{:S(2)}) collective-permute-start(f32[8,128]{1,0:T(8,128)S(1)} %add.326), channel_id=1, source_target_pairs={{0,64},{8,72},{16,80},{24,88},{32,96},{40,104},{48,112},{56,120},{... | collective-permute-start | bytes 12296 | tf_op jit(solution)/shard_map/ppermute | solution.py:390
  178.5 5.1 %collective-permute-start.16 = (f32[8,128]{1,0:T(8,128)S(1)}, f32[8,128]{1,0:T(8,128)S(1)}, u32[]{:S(2)}, u32[]{:S(2)}) collective-permute-start(f32[8,128]{1,0:T(8,128)S(1)} %add.327), channel_id=1, source_target_pairs={{0,128},{8,136},{16,144},{24,152},{32,160},{40,168},{48,176},{56,1... | collective-permute-start | bytes 12296 | tf_op jit(solution)/shard_map/ppermute | solution.py:391
  187.3 5.1 %collective-permute-start.18 = (f32[8,128]{1,0:T(8,128)S(1)}, f32[8,128]{1,0:T(8,128)S(1)}, u32[]{:S(2)}, u32[]{:S(2)}) collective-permute-start(f32[8,128]{1,0:T(8,128)S(1)} %add.329), channel_id=1, source_target_pairs={{0,32},{8,40},{16,48},{24,56},{32,0},{40,8},{48,16},{56,24},{64,96... | collective-permute-start | bytes 12296 | tf_op jit(solution)/shard_map/ppermute | solution.py:393
  194.5 8.7 %collective-permute-start.28 = (bf16[64,1024]{1,0:T(8,128)(2,1)S(1)}, bf16[64,1024]{1,0:T(8,128)(2,1)S(1)}, u32[]{:S(2)}, u32[]{:S(2)}) collective-permute-start(bf16[64,1024]{1,0:T(8,128)(2,1)S(1)} %get-tuple-element.89), channel_id=1, source_target_pairs={{0,128},{8,136},{16,144},{24,152},{32,160},{40,168},{48,176},{56,1... | collective-permute-start | bytes 393224 | tf_op jit(solution)/shard_map/ppermute | solution.py:321
  194.9 8.3 %collective-permute-start.29 = (bf16[64,1024]{1,0:T(8,128)(2,1)S(1)}, bf16[64,1024]{1,0:T(8,128)(2,1)S(1)}, u32[]{:S(2)}, u32[]{:S(2)}) collective-permute-start(bf16[64,1024]{1,0:T(8,128)(2,1)S(1)} %get-tuple-element.91), channel_id=1, source_target_pairs={{0,64},{8,72},{16,80},{24,88},{32,96},{40,104},{48,112},{56,120},{... | collective-permute-start | bytes 393224 | tf_op jit(solution)/shard_map/ppermute | solution.py:321
  196.7 6.5 %collective-permute-start.30 = (bf16[64,1024]{1,0:T(8,128)(2,1)S(1)}, bf16[64,1024]{1,0:T(8,128)(2,1)S(1)}, u32[]{:S(2)}, u32[]{:S(2)}) collective-permute-start(bf16[64,1024]{1,0:T(8,128)(2,1)S(1)} %get-tuple-element.90), channel_id=1, source_target_pairs={{0,192},{8,200},{16,208},{24,216},{32,224},{40,232},{48,240},{56,2... | collective-permute-start | bytes 393224 | tf_op jit(solution)/shard_map/ppermute | solution.py:321
  198.5 6.6 %collective-permute-start.22 = (bf16[64,1024]{1,0:T(8,128)(2,1)S(1)}, bf16[64,1024]{1,0:T(8,128)(2,1)S(1)}, u32[]{:S(2)}, u32[]{:S(2)}) collective-permute-start(bf16[64,1024]{1,0:T(8,128)(2,1)S(1)} %get-tuple-element.92), channel_id=1, source_target_pairs={{0,32},{8,40},{16,48},{24,56},{32,0},{40,8},{48,16},{56,24},{64,96... | collective-permute-start | bytes 393224 | tf_op jit(solution)/shard_map/ppermute | solution.py:321
  200.2 5.5 %collective-permute-start.23 = (bf16[64,1024]{1,0:T(8,128)(2,1)S(1)}, bf16[64,1024]{1,0:T(8,128)(2,1)S(1)}, u32[]{:S(2)}, u32[]{:S(2)}) collective-permute-start(bf16[64,1024]{1,0:T(8,128)(2,1)S(1)} %get-tuple-element.94), channel_id=1, source_target_pairs={{0,16},{8,24},{16,32},{24,40},{32,48},{40,56},{48,0},{56,8},{64,80... | collective-permute-start | bytes 393224 | tf_op jit(solution)/shard_map/ppermute | solution.py:321
  203.2 6.2 %collective-permute-start.24 = (bf16[64,1024]{1,0:T(8,128)(2,1)S(1)}, bf16[64,1024]{1,0:T(8,128)(2,1)S(1)}, u32[]{:S(2)}, u32[]{:S(2)}) collective-permute-start(bf16[64,1024]{1,0:T(8,128)(2,1)S(1)} %get-tuple-element.93), channel_id=1, source_target_pairs={{0,48},{8,56},{16,0},{24,8},{32,16},{40,24},{48,32},{56,40},{64,11... | collective-permute-start | bytes 393224 | tf_op jit(solution)/shard_map/ppermute | solution.py:321
  (10 other events, 110.8 us)
Sparse Core Ops, SparseCore 0:
  11.2 60.8 all-gather.1
  132.5 39.5 reduce-scatter.1
